TPU v7x, 32 devices: a whole 2x2x4 slice. The times are simulated.
32 devices in a mesh: groups: 2 (over x), tensor: 16 (over z, y, core).
Axes of the slice: x: 2, y: 2, z: 4, core: 2. Of those that a mesh axis runs over, the one named last changes fastest.
Arguments:
- tokens: bfloat16 [256, 4096], P(('groups', 'tensor')), parts along dimension 0, may hold values from -6 to 6
- cotangent: bfloat16 [256, 4096], P(('groups', 'tensor')), parts along dimension 0, may hold values from -6 to 6
- gate_weight: bfloat16 [4096, 16384], P(None, 'tensor'), may hold values from -0.09375 to 0.09375
- up_weight: bfloat16 [4096, 16384], P(None, 'tensor'), may hold values from -0.09375 to 0.09375
- down_weight: bfloat16 [16384, 4096], P('tensor'), may hold values from -0.046875 to 0.046875
- gate_mask: int32 [32, 128], P(None, 'tensor'), may hold values from 0 to 1, as said below
- up_mask: int32 [32, 128], P(None, 'tensor'), may hold values from 0 to 1, as said below
- down_mask: int32 [128, 32], P('tensor'), may hold values from 0 to 1, as said below
Outputs:
- mixed: bfloat16 [256, 4096], P(('groups', 'tensor')), parts along dimension 0
- grad_tokens: bfloat16 [256, 4096], P(('groups', 'tensor')), parts along dimension 0
- grad_gate: bfloat16 [8192, 16384], P('groups', 'tensor'), parts along dimension 0
- grad_up: bfloat16 [8192, 16384], P('groups', 'tensor'), parts along dimension 0
- grad_down: bfloat16 [32768, 4096], P(('groups', 'tensor')), parts along dimension 0
There are 2 independent parts, one for each index of `groups`. A program takes and returns all parts, laid end to end along the dimension named above; an argument that names none is the same for every part. Nothing has to cross between parts.
Inputs may be any that keep to these rules, and one draw needn't show every extreme that they name: `gate_mask`: 0 or 1; the share of kept blocks differs from one column of blocks of hidden units to another. `up_mask`: 0 or 1; the share of kept blocks differs from one column of blocks of hidden units to another. `down_mask`: 0 or 1; the share of kept blocks differs from one row of blocks of hidden units to another.
All inputs are finite; a program needn't handle non-finite values.
Results may differ from a plain program's by a relative error of at most 0.0049.
Values may be sent and summed in bfloat16 or wider, within the bound.
A program may use at most 192 MiB of HBM per device.

v0:
```python
import functools

import jax
import jax.numpy as jnp
from jax import lax
from jax.experimental import pallas as pl
from jax.experimental.pallas import tpu as pltpu
from jax.sharding import PartitionSpec as P

BLK = 128
CHUNKS = 4
F32 = jnp.float32
BF16 = jnp.bfloat16


def dot(left, right, left_dim=1, right_dim=0):
    return lax.dot_general(
        left, right, (((left_dim,), (right_dim,)), ((), ())), preferred_element_type=F32
    )


def spread_lanes(mask, out):
    rows, cols = mask.shape
    for j in range(cols):
        out[:, j * BLK:(j + 1) * BLK] = jnp.broadcast_to(
            mask[:, j:j + 1].astype(F32), (rows, BLK)
        )


def masked(block, row):
    cols = block.shape[1]
    wide = jnp.broadcast_to(row, (16, cols)).astype(BF16)
    return (block.reshape(BLK // 16, 16, cols) * wide[None]).reshape(BLK, cols)


def exchange_kernel(
    m, tok, cot, gm, um, dm, gw_h, uw_h, dw_h,
    mixed_o, gt_o, xw, cw, hid, ggp, gup, eg, eu, ed,
    gw, uw, dw, tbuf, cbuf, gate, up, gh, gs, du,
    pb, ra, rb, bb, cb, rz, wsem, send_sem, recv_sem,
):
    n = 4 * m
    per, d = tok.shape
    half = d // 2
    hidden = gate.shape[1]
    total = gate.shape[0]
    kc_n = wsem.shape[1]
    kc = d // kc_n
    width = d // CHUNKS
    h = width // 2
    group = lax.axis_index("groups")
    t = lax.axis_index("tensor")
    c, y, z = lax.rem(t, 2), lax.rem(t // 2, 2), t // 4

    def device(cc, yy, zz):
        return (group, zz * 4 + yy * 2 + cc)

    def gate_copy(k):
        rows = pl.ds(pl.multiple_of(k * kc, kc), kc)
        return pltpu.make_async_copy(gw_h.at[rows, :], gw.at[rows, :], wsem.at[0, k])

    def up_copy(k):
        rows = pl.ds(pl.multiple_of(k * kc, kc), kc)
        return pltpu.make_async_copy(uw_h.at[rows, :], uw.at[rows, :], wsem.at[1, k])

    def down_copy(k):
        return pltpu.make_async_copy(
            dw_h.at[:, pl.ds(k * width, width)], dw.at[k], wsem.at[2, k]
        )

    for k in range(kc_n):
        gate_copy(k).start()
        up_copy(k).start()
    for k in range(CHUNKS):
        down_copy(k).start()

    z_peers = [lax.rem(z + off, m) for off in range(m)]
    z_from = [lax.rem(z - off + m, m) for off in range(m)]
    y_peer = device(c, 1 - y, z)
    c_peer = device(1 - c, y, z)

    barrier = pltpu.get_barrier_semaphore()
    peers = [device(c, y, z_peers[off]) for off in range(1, m)] + [y_peer, c_peer]
    for peer in peers:
        pl.semaphore_signal(barrier, inc=1, device_id=peer, device_id_type=pl.DeviceIdType.MESH)

    def own_slab(src, buf):
        v = src[...].astype(F32)
        buf[c, y, z] = jnp.concatenate([v[:, :half], v[:, half:]], axis=0).astype(BF16)

    own_slab(tok, tbuf)
    own_slab(cot, cbuf)
    spread_lanes(gm, eg)
    spread_lanes(um, eu)
    spread_lanes(dm, ed)
    pl.semaphore_wait(barrier, len(peers))

    counter = [0]
    sent = []

    def remote(src, dst, peer):
        i = counter[0]
        counter[0] += 1
        copy = pltpu.make_async_remote_copy(
            src_ref=src, dst_ref=dst, send_sem=send_sem.at[i], recv_sem=recv_sem.at[i],
            device_id=peer, device_id_type=pl.DeviceIdType.MESH,
        )
        sent.append(copy)
        return copy

    def gather(buf):
        own = buf.at[c, y, z]
        zc = [remote(own, own, device(c, y, z_peers[off])) for off in range(1, m)]
        yc = [remote(buf.at[c, y, s], buf.at[c, y, s], y_peer) for s in z_from]
        cc = [
            [remote(buf.at[c, yy, s], buf.at[c, yy, s], c_peer) for s in z_from]
            for yy in (y, 1 - y)
        ]

        def begin():
            for copy in zc:
                copy.start()
            yc[0].start()
            cc[0][0].start()

        def forward():
            for off in range(1, m):
                zc[off - 1].wait_recv()
                yc[off].start()
                cc[0][off].start()

        def across():
            for off in range(m):
                yc[off].wait_recv()
                cc[1][off].start()

        def end():
            for row in cc:
                for copy in row:
                    copy.wait_recv()

        return begin, forward, across, end

    def unpack(buf, out):
        for p in range(n // 2):
            a, b = (buf[q // (2 * m), (q // m) % 2, q % m].astype(F32) for q in (2 * p, 2 * p + 1))
            rows = slice(2 * per * p, 2 * per * (p + 1))
            out[rows, :half] = jnp.concatenate([a[:per], b[:per]], axis=0).astype(BF16)
            out[rows, half:] = jnp.concatenate([a[per:], b[per:]], axis=0).astype(BF16)

    t_begin, t_forward, t_across, t_end = gather(tbuf)
    c_begin, c_forward, c_across, c_end = gather(cbuf)
    t_begin()
    t_forward()
    c_begin()
    t_across()
    t_end()
    unpack(tbuf, xw)
    gate[...] = jnp.zeros_like(gate)
    up[...] = jnp.zeros_like(up)

    def first(k, carry):
        cols = pl.ds(pl.multiple_of(k * kc, kc), kc)
        gate_copy(k).wait()
        up_copy(k).wait()
        x = xw[:, cols]
        for w, e, acc in ((gw, eg, gate), (uw, eu, up)):
            for b in range(kc // BLK):
                rows = pl.ds(pl.multiple_of(k * kc + b * BLK, BLK), BLK)
                w[rows, :] = masked(w[rows, :], e[pl.ds(k * (kc // BLK) + b, 1), :])
            acc[...] += dot(x, w[cols, :])
        return carry

    lax.fori_loop(0, kc_n // 2, first, 0)
    c_forward()
    lax.fori_loop(kc_n // 2, kc_n, first, 0)
    c_across()

    step = 32

    def middle(k, carry):
        rows = pl.ds(pl.multiple_of(k * step, step), step)
        g, u = gate[rows, :], up[rows, :]
        s = jax.nn.sigmoid(g)
        a = g * s
        gs[rows, :] = a
        hid[rows, :] = (a * u).astype(BF16)
        du[rows, :] = u * s * (1.0 + g * (1.0 - s))
        return carry

    lax.fori_loop(0, total // step, middle, 0)
    c_end()
    unpack(cbuf, cw)

    sums = []

    def scatter_begin(which, k, low, high):
        parts = jnp.concatenate([low.reshape(n, per, h), high.reshape(n, per, h)], axis=1)
        pb[which, k] = parts.astype(BF16).reshape(2, 2, m, 2 * per, h)
        a = remote(pb.at[which, k, 1 - c], ra.at[which, k], c_peer)
        b = remote(bb.at[which, k], rb.at[which, k], y_peer)
        zs = [
            remote(cb.at[which, k, z_peers[off]], rz.at[which, k, off - 1], device(c, y, z_peers[off]))
            for off in range(1, m)
        ]
        a.start()

        def second():
            a.wait_recv()
            bb[which, k] = (pb[which, k, c, 1 - y].astype(F32) + ra[which, k, 1 - y].astype(F32)).astype(BF16)
            b.start()

        def third():
            b.wait_recv()
            cb[which, k] = (
                pb[which, k, c, y].astype(F32) + ra[which, k, y].astype(F32) + rb[which, k].astype(F32)
            ).astype(BF16)
            for copy in zs:
                copy.start()

        def last():
            value = (
                pb[which, k, c, y, z].astype(F32) + ra[which, k, y, z].astype(F32) + rb[which, k, z].astype(F32)
            )
            for off in range(1, m):
                zs[off - 1].wait_recv()
                value = value + rz[which, k, off - 1].astype(F32)
            out = gt_o if which else mixed_o
            out[:, k * width:k * width + h] = value[:per].astype(BF16)
            out[:, k * width + h:(k + 1) * width] = value[per:].astype(BF16)

        sums.append((second, third, last))

    def advance(i):
        for stage in range(3):
            j = i - 1 - stage
            if 0 <= j < 2 * CHUNKS:
                sums[j][stage]()

    for k in range(CHUNKS):
        down_copy(k).wait()
        cols = slice(k * width, (k + 1) * width)
        for j in range(hidden // BLK):
            rows = slice(j * BLK, (j + 1) * BLK)
            dw[k, rows, :] = masked(dw[k, rows, :], ed[j:j + 1, cols])
        hv = hid[...]
        scatter_begin(0, k, dot(hv, dw[k, :, :h]), dot(hv, dw[k, :, h:]))
        value = dot(cw[:, cols], dw[k], 1, 1)
        gh[...] = value if k == 0 else gh[...] + value
        advance(k)

    def pre(k, carry):
        rows = pl.ds(pl.multiple_of(k * step, step), step)
        g = gh[rows, :]
        ggp[rows, :] = (g * du[rows, :]).astype(BF16)
        gup[rows, :] = (g * gs[rows, :]).astype(BF16)
        return carry

    lax.fori_loop(0, total // step, pre, 0)

    for k in range(CHUNKS):
        a, b = ggp[...], gup[...]
        halves = []
        for o in (k * width, k * width + h):
            halves.append(dot(a, gw[o:o + h, :], 1, 1) + dot(b, uw[o:o + h, :], 1, 1))
        scatter_begin(1, k, *halves)
        advance(CHUNKS + k)
    for i in range(2 * CHUNKS, 2 * CHUNKS + 4):
        advance(i)
    for copy in sent:
        copy.wait_send()


def grads_kernel(xw, cw, hid, ggp, gup, eg, eu, ed, gg, gu, gd):
    i = pl.program_id(0)
    block = xw.shape[1]
    for pre, e, out in ((ggp, eg, gg), (gup, eu, gu)):
        for b in range(block // BLK):
            rows = slice(b * BLK, (b + 1) * BLK)
            value = dot(xw[:, rows], pre[...], 0, 0)
            out[rows, :] = (value * e[pl.ds(i * (block // BLK) + b, 1), :]).astype(BF16)
    for j in range(hid.shape[1] // BLK):
        rows = slice(j * BLK, (j + 1) * BLK)
        value = dot(hid[:, rows], cw[...], 0, 0)
        gd[rows, :] = (value * ed[j:j + 1, :]).astype(BF16)


def shards(n, tokens, cotangent, gate_weight, up_weight, down_weight, gate_mask, up_mask, down_mask):
    m = n // 4
    per, d = tokens.shape
    total = n * per
    hidden = gate_weight.shape[1]
    width = d // CHUNKS
    h = width // 2
    kc_n = 8
    copies = 2 * (m - 1 + 3 * m) + 2 * CHUNKS * (m + 1)
    vmem = pl.BlockSpec(memory_space=pltpu.VMEM)
    hbm = pl.BlockSpec(memory_space=pl.ANY)
    shape = jax.ShapeDtypeStruct
    mixed, grad_tokens, xw, cw, hid, ggp, gup, eg, eu, ed = pl.pallas_call(
        functools.partial(exchange_kernel, m),
        out_shape=(
            shape((per, d), BF16), shape((per, d), BF16),
            shape((total, d), BF16), shape((total, d), BF16),
            shape((total, hidden), BF16), shape((total, hidden), BF16), shape((total, hidden), BF16),
            shape((d // BLK, hidden), F32), shape((d // BLK, hidden), F32),
            shape((hidden // BLK, d), F32),
        ),
        in_specs=[vmem] * 5 + [hbm] * 3,
        out_specs=(vmem,) * 10,
        scratch_shapes=[
            pltpu.VMEM((d, hidden), BF16), pltpu.VMEM((d, hidden), BF16),
            pltpu.VMEM((CHUNKS, hidden, width), BF16),
            pltpu.VMEM((2, 2, m, 2 * per, d // 2), BF16), pltpu.VMEM((2, 2, m, 2 * per, d // 2), BF16),
            *[pltpu.VMEM((total, hidden), F32)] * 5,
            pltpu.VMEM((2, CHUNKS, 2, 2, m, 2 * per, h), BF16),
            pltpu.VMEM((2, CHUNKS, 2, m, 2 * per, h), BF16),
            pltpu.VMEM((2, CHUNKS, m, 2 * per, h), BF16),
            pltpu.VMEM((2, CHUNKS, m, 2 * per, h), BF16),
            pltpu.VMEM((2, CHUNKS, m, 2 * per, h), BF16),
            pltpu.VMEM((2, CHUNKS, m - 1, 2 * per, h), BF16),
            pltpu.SemaphoreType.DMA((3, kc_n)),
            pltpu.SemaphoreType.DMA((copies,)),
            pltpu.SemaphoreType.DMA((copies,)),
        ],
        compiler_params=pltpu.CompilerParams(
            collective_id=0, has_side_effects=True, vmem_limit_bytes=60 * 2**20
        ),
        cost_estimate=pl.CostEstimate(
            flops=12 * total * d * hidden, bytes_accessed=6 * d * hidden, transcendentals=total * hidden
        ),
    )(tokens, cotangent, gate_mask, up_mask, down_mask, gate_weight, up_weight, down_weight)

    block = 512
    whole = lambda *dims: pl.BlockSpec(dims, lambda i: (0, 0))
    grad_gate, grad_up, grad_down = pl.pallas_call(
        grads_kernel,
        grid=(d // block,),
        out_shape=(shape((d, hidden), BF16), shape((d, hidden), BF16), shape((hidden, d), BF16)),
        in_specs=[
            pl.BlockSpec((total, block), lambda i: (0, i)),
            pl.BlockSpec((total, block), lambda i: (0, i)),
            whole(total, hidden), whole(total, hidden), whole(total, hidden),
            whole(d // BLK, hidden), whole(d // BLK, hidden),
            pl.BlockSpec((hidden // BLK, block), lambda i: (0, i)),
        ],
        out_specs=(
            pl.BlockSpec((block, hidden), lambda i: (i, 0)),
            pl.BlockSpec((block, hidden), lambda i: (i, 0)),
            pl.BlockSpec((hidden, block), lambda i: (0, i)),
        ),
        compiler_params=pltpu.CompilerParams(vmem_limit_bytes=32 * 2**20),
        cost_estimate=pl.CostEstimate(
            flops=6 * total * d * hidden, bytes_accessed=6 * d * hidden, transcendentals=0
        ),
    )(xw, cw, hid, ggp, gup, eg, eu, ed)
    return mixed, grad_tokens, grad_gate, grad_up, grad_down


def solution(mesh):
    return jax.shard_map(
        functools.partial(shards, mesh.shape["tensor"]),
        mesh=mesh,
        in_specs=(
            P(("groups", "tensor"), None),
            P(("groups", "tensor"), None),
            P(None, "tensor"),
            P(None, "tensor"),
            P("tensor", None),
            P(None, "tensor"),
            P(None, "tensor"),
            P("tensor", None),
        ),
        out_specs=(
            P(("groups", "tensor"), None),
            P(("groups", "tensor"), None),
            P("groups", "tensor"),
            P("groups", "tensor"),
            P(("groups", "tensor"), None),
        ),
        check_vma=False,
    )
```

profile of v0, /device:TPU:0, one launch (start us, length us, event | category | flops | bytes accessed | tf_op | source)
XLA Modules:
  0.0 82.5 jit_solution(6231859841687448919)
XLA Ops:
  0.6 1.4 %copy.13.gm = s32[32,8]{1,0:T(8,128)} copy(s32[32,8]{0,1:T(8,128)} %param.13) | data formatting | bytes 2048 | tf_op args[5]
  2.0 1.4 %copy.14.um = s32[32,8]{1,0:T(8,128)} copy(s32[32,8]{0,1:T(8,128)} %param.14) | data formatting | bytes 2048 | tf_op args[6]
  3.4 59.6 %shard_map.119 = (bf16[8,4096]{1,0:T(8,128)(2,1)}, bf16[8,4096]{1,0:T(8,128)(2,1)}, bf16[128,4096]{1,0:T(8,128)(2,1)}, bf16[128,4096]{1,0:T(8,128)(2,1)}, bf16[1...) custom-call(bf16[8,4096]{1,0:T(8,128)(2,1)} %tok.1, ...), custom_call_target="tpu_custom_call" | custom-call | flops 6442450944 | bytes 25165824 | tf_op jit(solution)/shard_map/pallas_call | solution.py:300
  63.0 0.0 copy-start
  63.0 1.2 %copy-done = bf16[128,4096]{1,0:T(8,128)(2,1)S(1)} copy-done((bf16[128,4096]{1,0:T(8,128)(2,1)S(1)}, bf16[128,4096]{1,0:T(8,128)(2,1)}, u32[]{:S(2)}) %copy-start) | copy-done | bytes 1048600
  64.2 0.0 copy-start.1
  64.2 1.2 %copy-done.1 = bf16[128,4096]{1,0:T(8,128)(2,1)S(1)} copy-done((bf16[128,4096]{1,0:T(8,128)(2,1)S(1)}, bf16[128,4096]{1,0:T(8,128)(2,1)}, u32[]{:S(2)}) %copy-start.1) | copy-done | bytes 1048600
  65.4 0.0 copy-start.2
  65.4 0.9 %copy-done.2 = bf16[128,1024]{1,0:T(8,128)(2,1)S(1)} copy-done((bf16[128,1024]{1,0:T(8,128)(2,1)S(1)}, bf16[128,1024]{1,0:T(8,128)(2,1)}, u32[]{:S(2)}) %copy-start.2) | copy-done | bytes 262168
  66.4 0.0 copy-start.3
  66.4 0.9 %copy-done.3 = bf16[128,1024]{1,0:T(8,128)(2,1)S(1)} copy-done((bf16[128,1024]{1,0:T(8,128)(2,1)S(1)}, bf16[128,1024]{1,0:T(8,128)(2,1)}, u32[]{:S(2)}) %copy-start.3) | copy-done | bytes 262168
  67.3 0.0 copy-start.4
  67.3 0.9 %copy-done.4 = bf16[128,1024]{1,0:T(8,128)(2,1)S(1)} copy-done((bf16[128,1024]{1,0:T(8,128)(2,1)S(1)}, bf16[128,1024]{1,0:T(8,128)(2,1)}, u32[]{:S(2)}) %copy-start.4) | copy-done | bytes 262168
  68.3 0.0 copy-start.5
  68.3 0.9 %copy-done.5 = f32[32,1024]{1,0:T(8,128)S(1)} copy-done((f32[32,1024]{1,0:T(8,128)S(1)}, f32[32,1024]{1,0:T(8,128)}, u32[]{:S(2)}) %copy-start.5) | copy-done | bytes 131096
  69.2 0.0 copy-start.6
  69.2 0.9 %copy-done.6 = f32[32,1024]{1,0:T(8,128)S(1)} copy-done((f32[32,1024]{1,0:T(8,128)S(1)}, f32[32,1024]{1,0:T(8,128)}, u32[]{:S(2)}) %copy-start.6) | copy-done | bytes 131096
  70.1 0.0 copy-start.7
  70.1 0.9 %copy-done.7 = f32[8,4096]{1,0:T(8,128)S(1)} copy-done((f32[8,4096]{1,0:T(8,128)S(1)}, f32[8,4096]{1,0:T(8,128)}, u32[]{:S(2)}) %copy-start.7) | copy-done | bytes 131096
  71.0 0.0 copy-start.9
  71.0 0.0 copy-start.8
  71.0 10.2 %shard_map.120 = (bf16[4096,1024]{1,0:T(8,128)(2,1)}, bf16[4096,1024]{1,0:T(8,128)(2,1)}, bf16[1024,4096]{1,0:T(8,128)(2,1)}) custom-call(bf16[128,4096]{1,0:T(8,128)(2,1)S(1)} %copy-done, bf16[128,4096]{1,0:T(8,128)(2,1)S(1)} %copy-done.1, bf16[128,1024]{1,0:T(8,128)(2,1)S(1)} %copy-done.2, bf16[128,1024]{1,0:T(8,128)(2,1)S(1)} %copy-done.3, ...), custom_call_target="tpu_custom_call" | custom-call | flops 3221225472 | bytes 25165824 | tf_op jit(solution)/shard_map/pallas_call | solution.py:336
  81.2 0.0 copy-done.9
  81.2 0.6 copy.17
  81.8 0.0 copy-done.8
  81.8 0.6 copy.18
Async XLA Ops:
  63.0 1.2 %copy-start = (bf16[128,4096]{1,0:T(8,128)(2,1)S(1)}, bf16[128,4096]{1,0:T(8,128)(2,1)}, u32[]{:S(2)}) copy-start(bf16[128,4096]{1,0:T(8,128)(2,1)} %get-tuple-element.20.xw) | copy-start | bytes 3145732
  64.2 1.2 %copy-start.1 = (bf16[128,4096]{1,0:T(8,128)(2,1)S(1)}, bf16[128,4096]{1,0:T(8,128)(2,1)}, u32[]{:S(2)}) copy-start(bf16[128,4096]{1,0:T(8,128)(2,1)} %get-tuple-element.21.cw) | copy-start | bytes 3145732
  65.4 0.9 %copy-start.2 = (bf16[128,1024]{1,0:T(8,128)(2,1)S(1)}, bf16[128,1024]{1,0:T(8,128)(2,1)}, u32[]{:S(2)}) copy-start(bf16[128,1024]{1,0:T(8,128)(2,1)} %get-tuple-element.22.hid) | copy-start | bytes 786436
  66.4 0.9 %copy-start.3 = (bf16[128,1024]{1,0:T(8,128)(2,1)S(1)}, bf16[128,1024]{1,0:T(8,128)(2,1)}, u32[]{:S(2)}) copy-start(bf16[128,1024]{1,0:T(8,128)(2,1)} %get-tuple-element.23.ggp) | copy-start | bytes 786436
  67.3 0.9 %copy-start.4 = (bf16[128,1024]{1,0:T(8,128)(2,1)S(1)}, bf16[128,1024]{1,0:T(8,128)(2,1)}, u32[]{:S(2)}) copy-start(bf16[128,1024]{1,0:T(8,128)(2,1)} %get-tuple-element.24.gup) | copy-start | bytes 786436
  68.3 0.9 %copy-start.5 = (f32[32,1024]{1,0:T(8,128)S(1)}, f32[32,1024]{1,0:T(8,128)}, u32[]{:S(2)}) copy-start(f32[32,1024]{1,0:T(8,128)} %get-tuple-element.25.eg) | copy-start | bytes 393220
  69.2 0.9 %copy-start.6 = (f32[32,1024]{1,0:T(8,128)S(1)}, f32[32,1024]{1,0:T(8,128)}, u32[]{:S(2)}) copy-start(f32[32,1024]{1,0:T(8,128)} %get-tuple-element.26.eu) | copy-start | bytes 393220
  70.1 0.9 %copy-start.7 = (f32[8,4096]{1,0:T(8,128)S(1)}, f32[8,4096]{1,0:T(8,128)}, u32[]{:S(2)}) copy-start(f32[8,4096]{1,0:T(8,128)} %get-tuple-element.27.ed) | copy-start | bytes 393220
  71.0 10.2 %copy-start.9 = (bf16[8,4096]{1,0:T(8,128)(2,1)S(1)}, bf16[8,4096]{1,0:T(8,128)(2,1)}, u32[]{:S(2)}) copy-start(bf16[8,4096]{1,0:T(8,128)(2,1)} %get-tuple-element.36) | copy-start | bytes 196612
  71.0 10.9 %copy-start.8 = (bf16[8,4096]{1,0:T(8,128)(2,1)S(1)}, bf16[8,4096]{1,0:T(8,128)(2,1)}, u32[]{:S(2)}) copy-start(bf16[8,4096]{1,0:T(8,128)(2,1)} %get-tuple-element.37) | copy-start | bytes 196612
where the time goes:
time: 82.9 us; the launch traced here: 82.5 us
  Pallas kernels  69.8 us (84%)
  local copies, waits for them, and re-layouts  12 us (14%)
    pallas_call x1, Pallas kernels, shards(): pl.pallas_call(functools.partial(exchange_kernel, m), out_shape=(shape((p...  59.6 us
    unnamed x24, local copies, waits for them, and re-layouts  12 us
    pallas_call x1, Pallas kernels, shards(): pl.pallas_call(grads_kernel, grid=(d // block,), out_shape=(shape((d, hid...  10.2 us

commit v1 on v0

--- a/solution.py
+++ b/solution.py
@@ -19,25 +19,17 @@
     )
 
 
-def spread_lanes(mask, out):
-    rows, cols = mask.shape
-    for j in range(cols):
-        out[:, j * BLK:(j + 1) * BLK] = jnp.broadcast_to(
-            mask[:, j:j + 1].astype(F32), (rows, BLK)
-        )
-
-
-def masked(block, row):
+def masked(block, keep):
     cols = block.shape[1]
-    wide = jnp.broadcast_to(row, (16, cols)).astype(BF16)
+    wide = jnp.concatenate([jnp.full((16, BLK), v, jnp.int32).astype(F32).astype(BF16) for v in keep], axis=1)
     return (block.reshape(BLK // 16, 16, cols) * wide[None]).reshape(BLK, cols)
 
 
 def exchange_kernel(
     m, tok, cot, gm, um, dm, gw_h, uw_h, dw_h,
-    mixed_o, gt_o, xw, cw, hid, ggp, gup, eg, eu, ed,
-    gw, uw, dw, tbuf, cbuf, gate, up, gh, gs, du,
-    pb, ra, rb, bb, cb, rz, wsem, send_sem, recv_sem,
+    mixed_o, gt_o, xw_o, cw_o, hid_o, ggp_o, gup_o,
+    xw, cw, hid, ggp, gup, gw, uw, dw, tbuf, cbuf, gate, up, gh, gs, du,
+    pb, ra, rb, bb, cb, rz, wsem, osem, send_sem, recv_sem,
 ):
     n = 4 * m
     per, d = tok.shape
@@ -90,10 +82,11 @@
 
     own_slab(tok, tbuf)
     own_slab(cot, cbuf)
-    spread_lanes(gm, eg)
-    spread_lanes(um, eu)
-    spread_lanes(dm, ed)
     pl.semaphore_wait(barrier, len(peers))
+
+    def save(i):
+        src, dst = ((xw, xw_o), (cw, cw_o), (hid, hid_o), (ggp, ggp_o), (gup, gup_o))[i]
+        return pltpu.make_async_copy(src, dst, osem.at[i])
 
     counter = [0]
     sent = []
@@ -156,6 +149,7 @@
     t_across()
     t_end()
     unpack(tbuf, xw)
+    save(0).start()
     gate[...] = jnp.zeros_like(gate)
     up[...] = jnp.zeros_like(up)
 
@@ -164,10 +158,12 @@
         gate_copy(k).wait()
         up_copy(k).wait()
         x = xw[:, cols]
-        for w, e, acc in ((gw, eg, gate), (uw, eu, up)):
+        for w, e, acc in ((gw, gm, gate), (uw, um, up)):
             for b in range(kc // BLK):
                 rows = pl.ds(pl.multiple_of(k * kc + b * BLK, BLK), BLK)
-                w[rows, :] = masked(w[rows, :], e[pl.ds(k * (kc // BLK) + b, 1), :])
+                w[rows, :] = masked(
+                    w[rows, :], [e[j, k * (kc // BLK) + b] for j in range(hidden // BLK)]
+                )
             acc[...] += dot(x, w[cols, :])
         return carry
 
@@ -191,6 +187,8 @@
     lax.fori_loop(0, total // step, middle, 0)
     c_end()
     unpack(cbuf, cw)
+    save(1).start()
+    save(2).start()
 
     sums = []
 
@@ -232,7 +230,7 @@
         sums.append((second, third, last))
 
     def advance(i):
-        for stage in range(3):
+        for stage in range(2):
             j = i - 1 - stage
             if 0 <= j < 2 * CHUNKS:
                 sums[j][stage]()
@@ -242,7 +240,9 @@
         cols = slice(k * width, (k + 1) * width)
         for j in range(hidden // BLK):
             rows = slice(j * BLK, (j + 1) * BLK)
-            dw[k, rows, :] = masked(dw[k, rows, :], ed[j:j + 1, cols])
+            dw[k, rows, :] = masked(
+                dw[k, rows, :], [dm[j, k * (width // BLK) + b] for b in range(width // BLK)]
+            )
         hv = hid[...]
         scatter_begin(0, k, dot(hv, dw[k, :, :h]), dot(hv, dw[k, :, h:]))
         value = dot(cw[:, cols], dw[k], 1, 1)
@@ -257,6 +257,8 @@
         return carry
 
     lax.fori_loop(0, total // step, pre, 0)
+    save(3).start()
+    save(4).start()
 
     for k in range(CHUNKS):
         a, b = ggp[...], gup[...]
@@ -265,24 +267,41 @@
             halves.append(dot(a, gw[o:o + h, :], 1, 1) + dot(b, uw[o:o + h, :], 1, 1))
         scatter_begin(1, k, *halves)
         advance(CHUNKS + k)
-    for i in range(2 * CHUNKS, 2 * CHUNKS + 4):
+    for i in range(2 * CHUNKS, 2 * CHUNKS + 2):
         advance(i)
+    for stages in sums:
+        stages[2]()
     for copy in sent:
         copy.wait_send()
-
-
-def grads_kernel(xw, cw, hid, ggp, gup, eg, eu, ed, gg, gu, gd):
+    for i in range(5):
+        save(i).wait()
+
+
+def grads_kernel(xw, cw, hid, ggp, gup, gm, um, dm, mixed, gt, gg, gu, gd, mixed_o, gt_o):
     i = pl.program_id(0)
     block = xw.shape[1]
-    for pre, e, out in ((ggp, eg, gg), (gup, eu, gu)):
-        for b in range(block // BLK):
+    count = block // BLK
+
+    @pl.when(i == 0)
+    def _():
+        mixed_o[...] = mixed[...]
+        gt_o[...] = gt[...]
+
+    def keep(value, scalars):
+        wide = [jnp.full((8, BLK), v, jnp.int32).astype(F32) for v in scalars]
+        wide = jnp.concatenate(wide, axis=1)
+        cols = wide.shape[1]
+        return (value.reshape(BLK // 8, 8, cols) * wide[None]).reshape(BLK, cols).astype(BF16)
+
+    for pre, e, out in ((ggp, gm, gg), (gup, um, gu)):
+        for b in range(count):
             rows = slice(b * BLK, (b + 1) * BLK)
             value = dot(xw[:, rows], pre[...], 0, 0)
-            out[rows, :] = (value * e[pl.ds(i * (block // BLK) + b, 1), :]).astype(BF16)
-    for j in range(hid.shape[1] // BLK):
+            out[rows, :] = keep(value, [e[j, i * count + b] for j in range(e.shape[0])])
+    for j in range(dm.shape[0]):
         rows = slice(j * BLK, (j + 1) * BLK)
         value = dot(hid[:, rows], cw[...], 0, 0)
-        gd[rows, :] = (value * ed[j:j + 1, :]).astype(BF16)
+        gd[rows, :] = keep(value, [dm[j, i * count + b] for b in range(count)])
 
 
 def shards(n, tokens, cotangent, gate_weight, up_weight, down_weight, gate_mask, up_mask, down_mask):
@@ -296,19 +315,20 @@
     copies = 2 * (m - 1 + 3 * m) + 2 * CHUNKS * (m + 1)
     vmem = pl.BlockSpec(memory_space=pltpu.VMEM)
     hbm = pl.BlockSpec(memory_space=pl.ANY)
+    smem = pl.BlockSpec(memory_space=pltpu.SMEM)
+    gate_mask, up_mask = gate_mask.T, up_mask.T
     shape = jax.ShapeDtypeStruct
-    mixed, grad_tokens, xw, cw, hid, ggp, gup, eg, eu, ed = pl.pallas_call(
+    mixed, grad_tokens, xw, cw, hid, ggp, gup = pl.pallas_call(
         functools.partial(exchange_kernel, m),
         out_shape=(
             shape((per, d), BF16), shape((per, d), BF16),
             shape((total, d), BF16), shape((total, d), BF16),
             shape((total, hidden), BF16), shape((total, hidden), BF16), shape((total, hidden), BF16),
-            shape((d // BLK, hidden), F32), shape((d // BLK, hidden), F32),
-            shape((hidden // BLK, d), F32),
-        ),
-        in_specs=[vmem] * 5 + [hbm] * 3,
-        out_specs=(vmem,) * 10,
+        ),
+        in_specs=[vmem] * 2 + [smem] * 3 + [hbm] * 3,
+        out_specs=(vmem,) * 2 + (hbm,) * 5,
         scratch_shapes=[
+            *[pltpu.VMEM((total, d), BF16)] * 2, *[pltpu.VMEM((total, hidden), BF16)] * 3,
             pltpu.VMEM((d, hidden), BF16), pltpu.VMEM((d, hidden), BF16),
             pltpu.VMEM((CHUNKS, hidden, width), BF16),
             pltpu.VMEM((2, 2, m, 2 * per, d // 2), BF16), pltpu.VMEM((2, 2, m, 2 * per, d // 2), BF16),
@@ -320,6 +340,7 @@
             pltpu.VMEM((2, CHUNKS, m, 2 * per, h), BF16),
             pltpu.VMEM((2, CHUNKS, m - 1, 2 * per, h), BF16),
             pltpu.SemaphoreType.DMA((3, kc_n)),
+            pltpu.SemaphoreType.DMA((5,)),
             pltpu.SemaphoreType.DMA((copies,)),
             pltpu.SemaphoreType.DMA((copies,)),
         ],
@@ -333,27 +354,28 @@
 
     block = 512
     whole = lambda *dims: pl.BlockSpec(dims, lambda i: (0, 0))
-    grad_gate, grad_up, grad_down = pl.pallas_call(
+    grad_gate, grad_up, grad_down, mixed, grad_tokens = pl.pallas_call(
         grads_kernel,
         grid=(d // block,),
-        out_shape=(shape((d, hidden), BF16), shape((d, hidden), BF16), shape((hidden, d), BF16)),
+        out_shape=(shape((d, hidden), BF16), shape((d, hidden), BF16), shape((hidden, d), BF16),
+                   shape((per, d), BF16), shape((per, d), BF16)),
         in_specs=[
             pl.BlockSpec((total, block), lambda i: (0, i)),
             pl.BlockSpec((total, block), lambda i: (0, i)),
             whole(total, hidden), whole(total, hidden), whole(total, hidden),
-            whole(d // BLK, hidden), whole(d // BLK, hidden),
-            pl.BlockSpec((hidden // BLK, block), lambda i: (0, i)),
+            smem, smem, smem, whole(per, d), whole(per, d),
         ],
         out_specs=(
             pl.BlockSpec((block, hidden), lambda i: (i, 0)),
             pl.BlockSpec((block, hidden), lambda i: (i, 0)),
             pl.BlockSpec((hidden, block), lambda i: (0, i)),
-        ),
-        compiler_params=pltpu.CompilerParams(vmem_limit_bytes=32 * 2**20),
+            whole(per, d), whole(per, d),
+        ),
+        compiler_params=pltpu.CompilerParams(vmem_limit_bytes=60 * 2**20),
         cost_estimate=pl.CostEstimate(
             flops=6 * total * d * hidden, bytes_accessed=6 * d * hidden, transcendentals=0
         ),
-    )(xw, cw, hid, ggp, gup, eg, eu, ed)
+    )(xw, cw, hid, ggp, gup, gate_mask, up_mask, down_mask, mixed, grad_tokens)
     return mixed, grad_tokens, grad_gate, grad_up, grad_down
 
 

time: 82.9 us -> 68.7 us (0.83)
  local copies, waits for them, and re-layouts: 12 us -> 0 us
  Pallas kernels: 69.8 us -> 67.7 us
    unnamed x24 -> x0, local copies, waits for them, and re-layouts: 12 us -> none
    pallas_call x1, Pallas kernels: 59.6 us -> 55.1 us  [shards(): pl.pallas_call(functools.partial(exchange_kernel, m), out_shape=(shape((p...]
    pallas_call x1, Pallas kernels: 10.2 us -> 12.6 us  [shards(): pl.pallas_call(grads_kernel, grid=(d // block,), out_shape=(shape((d, hid...]
where the time goes in v1:
time: 68.7 us; the launch traced here: 68.4 us
  Pallas kernels  67.7 us (99%)
    pallas_call x1, Pallas kernels, shards(): pl.pallas_call(functools.partial(exchange_kernel, m), out_shape=(shape((p...  55.1 us
    pallas_call x1, Pallas kernels, shards(): pl.pallas_call(grads_kernel, grid=(d // block,), out_shape=(shape((d, hid...  12.6 us

profile of v1, /device:TPU:0, one launch (start us, length us, event | category | flops | bytes accessed | tf_op | source)
XLA Modules:
  0.0 68.4 jit_solution(11130095885357064934)
XLA Ops:
  0.6 55.1 %shard_map.119 = (bf16[8,4096]{1,0:T(8,128)(2,1)}, bf16[8,4096]{1,0:T(8,128)(2,1)}, bf16[128,4096]{1,0:T(8,128)(2,1)}, bf16[128,4096]{1,0:T(8,128)(2,1)}, bf16[1...) custom-call(bf16[8,4096]{1,0:T(8,128)(2,1)} %tok.1, bf16[8,4096]{1,0:T(8,128)(2,1)} %cot.1, ...), custom_call_target="tpu_custom_call" | custom-call | flops 6442450944 | bytes 25165824 | tf_op jit(solution)/shard_map/pallas_call | solution.py:321
  55.8 12.6 %shard_map.120 = (bf16[4096,1024]{1,0:T(8,128)(2,1)}, bf16[4096,1024]{1,0:T(8,128)(2,1)}, bf16[1024,4096]{1,0:T(8,128)(2,1)}, bf16[8,4096]{1,0:T(8,128)(2,1)}, bf16[8,4096]{1,0:T(8,128)(2,1)}) custom-call(bf16[128,4096]{1,0:T(8,128)(2,1)} %get-tuple-element.17.xw, bf16[128,4096]{1,0:T(8,128)(2,1)} %get-tuple-element.18.cw, ...), custom_call_target="tpu_custom_call" | custom-call | flops 3221225472 | bytes 25165824 | tf_op jit(solution)/shard_map/pallas_call | solution.py:357

commit v2 on v1

--- a/solution.py
+++ b/solution.py
@@ -67,7 +67,6 @@
         down_copy(k).start()
 
     z_peers = [lax.rem(z + off, m) for off in range(m)]
-    z_from = [lax.rem(z - off + m, m) for off in range(m)]
     y_peer = device(c, 1 - y, z)
     c_peer = device(1 - c, y, z)
 
@@ -91,46 +90,78 @@
     counter = [0]
     sent = []
 
-    def remote(src, dst, peer):
+    def when(ok, act):
+        if ok is None:
+            act()
+        else:
+            pl.when(ok)(lambda: act())
+
+    def remote(src, dst, peer, ok=None):
         i = counter[0]
         counter[0] += 1
         copy = pltpu.make_async_remote_copy(
             src_ref=src, dst_ref=dst, send_sem=send_sem.at[i], recv_sem=recv_sem.at[i],
             device_id=peer, device_id_type=pl.DeviceIdType.MESH,
         )
-        sent.append(copy)
+        sent.append((copy, ok))
         return copy
 
+    right, left = device(c, y, jnp.minimum(z + 1, m - 1)), device(c, y, jnp.maximum(z - 1, 0))
+
     def gather(buf):
-        own = buf.at[c, y, z]
-        zc = [remote(own, own, device(c, y, z_peers[off])) for off in range(1, m)]
-        yc = [remote(buf.at[c, y, s], buf.at[c, y, s], y_peer) for s in z_from]
+        slabs = [(None, z)]
+        hops = {}
+        for s in range(1, m):
+            old_r, old_l = jnp.maximum(z - s + 1, 0), jnp.minimum(z + s - 1, m - 1)
+            going = None if s == 1 else z - s + 1 >= 0
+            coming = None if s == 1 else z + s - 1 < m
+            to_right = z + 1 < m if going is None else jnp.logical_and(z + 1 < m, going)
+            to_left = z >= 1 if coming is None else jnp.logical_and(z >= 1, coming)
+            hops[s] = (
+                remote(buf.at[c, y, old_r], buf.at[c, y, old_r], right, to_right), to_right,
+                remote(buf.at[c, y, old_l], buf.at[c, y, old_l], left, to_left), to_left,
+            )
+            slabs.append((z - s >= 0, jnp.maximum(z - s, 0)))
+            slabs.append((z + s < m, jnp.minimum(z + s, m - 1)))
+        yc = [remote(buf.at[c, y, s], buf.at[c, y, s], y_peer, ok) for ok, s in slabs]
         cc = [
-            [remote(buf.at[c, yy, s], buf.at[c, yy, s], c_peer) for s in z_from]
+            [remote(buf.at[c, yy, s], buf.at[c, yy, s], c_peer, ok) for ok, s in slabs]
             for yy in (y, 1 - y)
         ]
 
+        def hop(s):
+            if s < m:
+                when(hops[s][1], hops[s][0].start)
+                when(hops[s][3], hops[s][2].start)
+
         def begin():
-            for copy in zc:
-                copy.start()
+            hop(1)
             yc[0].start()
             cc[0][0].start()
 
         def forward():
-            for off in range(1, m):
-                zc[off - 1].wait_recv()
-                yc[off].start()
-                cc[0][off].start()
+            for s in range(1, m):
+                for way in range(2):
+                    i = 2 * s - 1 + way
+
+                    def arrive(i=i, s=s, way=way):
+                        hops[s][2 * way].wait_recv()
+
+                    when(slabs[i][0], arrive)
+                    if s + 1 < m:
+                        when(hops[s + 1][2 * way + 1], hops[s + 1][2 * way].start)
+                    when(slabs[i][0], yc[i].start)
+                    when(slabs[i][0], cc[0][i].start)
 
         def across():
-            for off in range(m):
-                yc[off].wait_recv()
-                cc[1][off].start()
+            for i, (ok, _) in enumerate(slabs):
+                when(ok, yc[i].wait_recv)
+                when(ok, cc[1][i].start)
 
         def end():
             for row in cc:
-                for copy in row:
-                    copy.wait_recv()
+                for copy, (ok, _) in zip(row, slabs):
+                    when(ok, copy.wait_recv)
 
         return begin, forward, across, end
 
@@ -147,6 +178,7 @@
     t_forward()
     c_begin()
     t_across()
+    c_forward()
     t_end()
     unpack(tbuf, xw)
     save(0).start()
@@ -168,9 +200,8 @@
         return carry
 
     lax.fori_loop(0, kc_n // 2, first, 0)
-    c_forward()
+    c_across()
     lax.fori_loop(kc_n // 2, kc_n, first, 0)
-    c_across()
 
     step = 32
 
@@ -271,8 +302,8 @@
         advance(i)
     for stages in sums:
         stages[2]()
-    for copy in sent:
-        copy.wait_send()
+    for copy, ok in sent:
+        when(ok, copy.wait_send)
     for i in range(5):
         save(i).wait()
 
@@ -312,7 +343,7 @@
     width = d // CHUNKS
     h = width // 2
     kc_n = 8
-    copies = 2 * (m - 1 + 3 * m) + 2 * CHUNKS * (m + 1)
+    copies = 2 * (8 * (m - 1) + 3) + 2 * CHUNKS * (m + 1)
     vmem = pl.BlockSpec(memory_space=pltpu.VMEM)
     hbm = pl.BlockSpec(memory_space=pl.ANY)
     smem = pl.BlockSpec(memory_space=pltpu.SMEM)
@@ -352,7 +383,7 @@
         ),
     )(tokens, cotangent, gate_mask, up_mask, down_mask, gate_weight, up_weight, down_weight)
 
-    block = 512
+    block = 256
     whole = lambda *dims: pl.BlockSpec(dims, lambda i: (0, 0))
     grad_gate, grad_up, grad_down, mixed, grad_tokens = pl.pallas_call(
         grads_kernel,

time: 68.7 us -> 78.4 us (1.14)
  Pallas kernels: 67.7 us -> 76.7 us
    pallas_call x1, Pallas kernels: 55.1 us -> 60.7 us  [shards(): pl.pallas_call(functools.partial(exchange_kernel, m), out_shape=(shape((p...]
    pallas_call x1, Pallas kernels: 12.6 us -> 16 us  [shards(): pl.pallas_call(grads_kernel, grid=(d // block,), out_shape=(shape((d, hid...]
where the time goes in v2:
time: 78.4 us; the launch traced here: 77.3 us
  Pallas kernels  76.7 us (98%)
    pallas_call x1, Pallas kernels, shards(): pl.pallas_call(functools.partial(exchange_kernel, m), out_shape=(shape((p...  60.7 us
    pallas_call x1, Pallas kernels, shards(): pl.pallas_call(grads_kernel, grid=(d // block,), out_shape=(shape((d, hid...  16 us

profile of v2, /device:TPU:0, one launch (start us, length us, event | category | flops | bytes accessed | tf_op | source)
XLA Modules:
  0.0 77.3 jit_solution(17608440749489210383)
XLA Ops:
  0.6 60.7 %shard_map.119 = (bf16[8,4096]{1,0:T(8,128)(2,1)}, bf16[8,4096]{1,0:T(8,128)(2,1)}, bf16[128,4096]{1,0:T(8,128)(2,1)}, bf16[128,4096]{1,0:T(8,128)(2,1)}, bf16[1...) custom-call(bf16[8,4096]{1,0:T(8,128)(2,1)} %tok.1, bf16[8,4096]{1,0:T(8,128)(2,1)} %cot.1, ...), custom_call_target="tpu_custom_call" | custom-call | flops 6442450944 | bytes 25165824 | tf_op jit(solution)/shard_map/pallas_call | solution.py:352
  61.3 16.0 %shard_map.120 = (bf16[4096,1024]{1,0:T(8,128)(2,1)}, bf16[4096,1024]{1,0:T(8,128)(2,1)}, bf16[1024,4096]{1,0:T(8,128)(2,1)}, bf16[8,4096]{1,0:T(8,128)(2,1)}, bf16[8,4096]{1,0:T(8,128)(2,1)}) custom-call(bf16[128,4096]{1,0:T(8,128)(2,1)} %get-tuple-element.17.xw, bf16[128,4096]{1,0:T(8,128)(2,1)} %get-tuple-element.18.cw, ...), custom_call_target="tpu_custom_call" | custom-call | flops 3221225472 | bytes 25165824 | tf_op jit(solution)/shard_map/pallas_call | solution.py:388
